TPU v7x, 32 devices: a whole 2x2x4 slice. The times are simulated.
32 devices in a mesh: rows: 16 (over z, y, x), layers: 2 (over core).
Axes of the slice: x: 2, y: 2, z: 4, core: 2. Of those that a mesh axis runs over, the one named last changes fastest.
Arguments:
- panel: float32 [8, 4096, 1024], P('layers', 'rows'), may hold values from -6 to 6, as said below
- factor: float32 [8, 4096, 2048], P(None, 'rows', 'layers'), may hold values from -4 to 4
Outputs:
- solved: float32 [8, 4096, 1024], P('layers', 'rows')
Inputs may be any that keep to these rules, and one draw needn't show every extreme that they name: The first 1024 rows of panel minus those rows of factor times the transpose of the first 1024 rows of factor form a symmetric positive definite block whose smallest eigenvalue is above 0.4.
All inputs are finite; a program needn't handle non-finite values.
Results may differ from a plain program's by a relative error of at most 0.00024.
Values sent between devices are 32-bit elements; how exact they have to be, the bound alone decides.
A program may use at most 128 MiB of HBM per device.

v0:
```python
import jax
import jax.numpy as jnp
from jax import lax
from jax.sharding import PartitionSpec as P


def spread(block, axis, holder):
    block = jnp.where(lax.axis_index(axis) == holder, block, jnp.zeros_like(block))
    return lax.psum(block, axis)


def shards(panel, factor):
    row_block = panel.shape[1]
    width = panel.shape[2]
    blocks = width // row_block
    own_cycles = panel.shape[0]
    layer_index = lax.axis_index("layers")
    pairs = [
        (spread(factor[0], "rows", owner), spread(panel[0], "rows", owner))
        for owner in range(blocks)
    ]
    target = jnp.concatenate([pair[0] for pair in pairs], 0)
    diag_input = jnp.concatenate([pair[1] for pair in pairs], 0)
    owned_diag = jnp.where(layer_index == 0, diag_input, jnp.zeros_like(diag_input))
    square = owned_diag - jnp.dot(
        target, target.T, precision=lax.Precision.HIGHEST, preferred_element_type=jnp.float32
    )
    diag_block = lax.psum(square, "layers")
    cycle_count = factor.shape[0]
    flat_rows = factor.reshape(cycle_count * row_block, factor.shape[2])
    product = jnp.dot(
        flat_rows, target.T, precision=lax.Precision.HIGHEST, preferred_element_type=jnp.float32
    )
    whole = lax.psum(product.reshape(cycle_count, row_block, width), "layers")
    summed = lax.dynamic_slice_in_dim(whole, layer_index * own_cycles, own_cycles, 0)
    reduced = panel - summed
    diag_factor = jnp.linalg.cholesky(diag_block)
    flat_reduced = reduced.reshape(-1, width)
    result = jax.scipy.linalg.solve_triangular(diag_factor, flat_reduced.T, lower=True).T
    return result.reshape(panel.shape)


def solution(mesh):
    in_specs = (P("layers", "rows", None), P(None, "rows", "layers"))
    out_specs = P("layers", "rows", None)
    return jax.shard_map(shards, mesh=mesh, in_specs=in_specs, out_specs=out_specs, check_vma=False)
```

profile of v0, /device:TPU:25, one launch (start us, length us, event | category | flops | bytes accessed | tf_op | source)
XLA Modules:
  0.0 821.9 jit_solution(6623526104286391113)
XLA Ops:
  12.1 282.1 %all-reduce.6.cloned.1.call-done = (f32[256,1024]{0,1:T(8,128)}, f32[256,1024]{0,1:T(8,128)}, f32[256,1024]{0,1:T(8,128)}, f32[256,1024]{0,1:T(8,128)}, f32[256,...) async-done(((f32[256,1024]{0,1:T(8,128)}, f32[256,1024]{0,1:T(8,128)}, f32[256,1024]{0,1:T(8,128)}, f32[256,1024]{0,1:T(8,128)}, ...) | async-done | bytes 8388624 | tf_op jit(solution)/shard_map/psum | solution.py:9
  299.4 55.7 %convolution_bitcast_fusion = f32[2048,1024]{0,1:T(8,128)} fusion(f32[1024,1024]{0,1:T(8,128)S(1)} %constant_dynamic-update-slice_fusion, f32[2048,1024]{1,0:T(8,128)} %bitcast.137), kind=kOutput, calls=%fused_computation.3 | convolution fusion | flops 25769803776 | bytes 20971520 | tf_op jit(solution)/shard_map/dot_general | solution.py:31
  355.1 9.4 %copy.32 = f32[2048,1024]{1,0:T(8,128)} copy(f32[2048,1024]{0,1:T(8,128)} %convolution_bitcast_fusion) | data formatting | bytes 16777216 | tf_op jit(solution)/shard_map/reshape | solution.py:34
  364.6 18.1 %fusion = f32[1024,1024]{0,1:T(8,128)} fusion(f32[256,1024]{0,1:T(8,128)S(1)} %copy-done.5, f32[256,1024]{0,1:T(8,128)S(1)} %copy-done.6, f32[256,1024]{0,1:T(8,128)S(1)} %copy-done.7, f32[256,1024]{0,1:T(8,128)} %get-tuple-element.32, pred[]{:T(512)S(6)} %eq.19, f32[1024,1024]{0,1:T(8,128)} %copy-done.4), kind=kOutput, calls=%fused_computation.5 | convolution fusion | flops 12890144768 | bytes 12582913 | tf_op jit(solution)/shard_map/dot_general | solution.py:25
  382.7 51.3 %all-reduce.8.cloned.1.call-done = (f32[8,256,1024]{2,1,0:T(8,128)}, f32[1024,1024]{0,1:T(8,128)}) async-done(((f32[8,256,1024]{2,1,0:T(8,128)}, f32[1024,1024]{0,1:T(8,128)}), (f32[8,256,1024]{2,1,0:T(8,128)}, f32[1024,1024]{0,1:T(8,128)})) %all-reduce.8.cloned.1.call-update) | async-done | bytes 12582928 | tf_op jit(solution)/shard_map/psum | solution.py:34
  434.1 5.5 copy.6
  439.6 4.4 fusion.1
  446.1 11.7 %cholesky.222 = f32[128,128]{1,0:T(8,128)S(1)} custom-call(f32[128,128]{1,0:T(8,128)S(1)} %cholesky.577), custom_call_target="Cholesky" | custom-call | tf_op jit(solution)/shard_map/jit(cholesky)/cholesky | solution.py:37
  457.9 9.8 %custom-call.63 = f32[1,128,128]{1,2,0:T(8,128)S(1)} custom-call(f32[1,128,128]{2,1,0:T(8,128)S(1)} %get-tuple-element.83), custom_call_target="InvertDiagBlocksLowerTriangular" | custom-call | tf_op jit(solution)/shard_map/jit(cholesky)/cholesky | solution.py:37
  471.1 11.7 %cholesky.243 = f32[128,128]{1,0:T(8,128)S(1)} custom-call(f32[128,128]{1,0:T(8,128)S(1)} %cholesky.581), custom_call_target="Cholesky" | custom-call | tf_op jit(solution)/shard_map/jit(cholesky)/cholesky | solution.py:37
  483.3 9.8 %custom-call.64 = f32[1,128,128]{1,2,0:T(8,128)S(1)} custom-call(f32[1,128,128]{2,1,0:T(8,128)S(1)} %get-tuple-element.81), custom_call_target="InvertDiagBlocksLowerTriangular" | custom-call | tf_op jit(solution)/shard_map/jit(cholesky)/cholesky | solution.py:37
  498.6 11.7 %cholesky.466 = f32[128,128]{1,0:T(8,128)S(1)} custom-call(f32[128,128]{1,0:T(8,128)S(1)} %cholesky.586), custom_call_target="Cholesky" | custom-call | tf_op jit(solution)/shard_map/jit(cholesky)/cholesky | solution.py:37
  511.1 9.8 %custom-call.65 = f32[1,128,128]{1,2,0:T(8,128)S(1)} custom-call(f32[1,128,128]{2,1,0:T(8,128)S(1)} %get-tuple-element.79), custom_call_target="InvertDiagBlocksLowerTriangular" | custom-call | tf_op jit(solution)/shard_map/jit(cholesky)/cholesky | solution.py:37
  525.5 11.7 %cholesky.485 = f32[128,128]{1,0:T(8,128)S(1)} custom-call(f32[128,128]{1,0:T(8,128)S(1)} %cholesky.591), custom_call_target="Cholesky" | custom-call | tf_op jit(solution)/shard_map/jit(cholesky)/cholesky | solution.py:37
  538.0 9.8 %custom-call.66 = f32[1,128,128]{1,2,0:T(8,128)S(1)} custom-call(f32[1,128,128]{2,1,0:T(8,128)S(1)} %get-tuple-element.77), custom_call_target="InvertDiagBlocksLowerTriangular" | custom-call | tf_op jit(solution)/shard_map/jit(cholesky)/cholesky | solution.py:37
  552.1 12.1 %cholesky.504 = f32[128,128]{1,0:T(8,128)S(1)} custom-call(f32[128,128]{1,0:T(8,128)S(1)} %cholesky.596), custom_call_target="Cholesky" | custom-call | tf_op jit(solution)/shard_map/jit(cholesky)/cholesky | solution.py:37
  565.0 9.8 %custom-call.67 = f32[1,128,128]{1,2,0:T(8,128)S(1)} custom-call(f32[1,128,128]{2,1,0:T(8,128)S(1)} %get-tuple-element.75), custom_call_target="InvertDiagBlocksLowerTriangular" | custom-call | tf_op jit(solution)/shard_map/jit(cholesky)/cholesky | solution.py:37
  579.2 11.7 %cholesky.524 = f32[128,128]{1,0:T(8,128)S(1)} custom-call(f32[128,128]{1,0:T(8,128)S(1)} %cholesky.601), custom_call_target="Cholesky" | custom-call | tf_op jit(solution)/shard_map/jit(cholesky)/cholesky | solution.py:37
  591.7 9.8 %custom-call.68 = f32[1,128,128]{1,2,0:T(8,128)S(1)} custom-call(f32[1,128,128]{2,1,0:T(8,128)S(1)} %get-tuple-element.73), custom_call_target="InvertDiagBlocksLowerTriangular" | custom-call | tf_op jit(solution)/shard_map/jit(cholesky)/cholesky | solution.py:37
  605.4 11.7 %cholesky.544 = f32[128,128]{1,0:T(8,128)S(1)} custom-call(f32[128,128]{1,0:T(8,128)S(1)} %cholesky.606), custom_call_target="Cholesky" | custom-call | tf_op jit(solution)/shard_map/jit(cholesky)/cholesky | solution.py:37
  617.9 9.8 %custom-call.69 = f32[1,128,128]{1,2,0:T(8,128)S(1)} custom-call(f32[1,128,128]{2,1,0:T(8,128)S(1)} %get-tuple-element.71), custom_call_target="InvertDiagBlocksLowerTriangular" | custom-call | tf_op jit(solution)/shard_map/jit(cholesky)/cholesky | solution.py:37
  630.8 11.7 %cholesky.562 = f32[128,128]{1,0:T(8,128)S(1)} custom-call(f32[128,128]{1,0:T(8,128)S(1)} %convolution_subtract_fusion.11), custom_call_target="Cholesky" | custom-call | tf_op jit(solution)/shard_map/jit(cholesky)/cholesky | solution.py:37
  653.7 4.9 select_select_fusion
  658.6 23.4 %while.1 = (s32[]{:T(128)}, f32[1024,1024]{0,1:T(8,128)}, s32[8,2]{0,1:T(2,128)S(1)}, f32[8,128,128]{2,1,0:T(8,128)S(1)}, s32[]{:T(128)}) while((s32[]{:T(128)}, f32[1024,1024]{0,1:T(8,128)}, s32[8,2]{0,1:T(2,128)S(1)}, f32[8,128,128]{2,1,0:T(8,128)S(1)}, s32[]{:T(128)}) %tuple.59), condition=%wide.while_cond, body=%wide.while_body.sunk | while | flops 2 | bytes 393329 | solution.py:39
  682.0 79.0 %custom-call.70 = f32[8,128,128]{1,2,0:T(8,128)S(1)} custom-call(f32[8,128,128]{2,1,0:T(8,128)S(1)} %get-tuple-element.12), custom_call_target="InvertDiagBlocksLowerTriangular" | custom-call | tf_op jit(solution)/shard_map/jit(_solve_triangular)/triangular_solve | solution.py:39
  761.0 4.4 dynamic-slice_subtract_fusion
  774.7 3.7 fusion.16
  780.0 4.6 fusion.19
  786.1 5.4 convolution_subtract_fusion.2
  793.0 6.1 convolution_subtract_fusion.1
  800.6 7.3 convolution_subtract_fusion.3
  809.5 5.3 copy.33
  (138 shorter events, 92.3 us)
Async XLA Ops:
  6.5 1.7 slice-start
  6.5 287.6 %all-reduce.6.cloned.1.call-start = ((), (), s32[]{:S(2)}) async-start(), calls=%async_computation | async-start | bytes 16777216 | tf_op jit(solution)/shard_map/psum | solution.py:9
  12.0 422.1 %all-reduce.8.cloned.1.call-start = ((), (), s32[]{:S(2)}) async-start(), calls=%async_computation.1 | async-start | bytes 25165824 | tf_op jit(solution)/shard_map/psum | solution.py:34
  294.2 2.9 copy-start.3
  294.2 3.1 copy-start.2
  297.4 2.0 copy-start.4
  355.1 9.5 %copy-start.5 = (f32[256,1024]{0,1:T(8,128)S(1)}, f32[256,1024]{0,1:T(8,128)}, u32[]{:S(2)}) copy-start(f32[256,1024]{0,1:T(8,128)} %get-tuple-element.29) | copy-start | bytes 3145732
  355.1 9.5 %copy-start.6 = (f32[256,1024]{0,1:T(8,128)S(1)}, f32[256,1024]{0,1:T(8,128)}, u32[]{:S(2)}) copy-start(f32[256,1024]{0,1:T(8,128)} %get-tuple-element.30) | copy-start | bytes 3145732
  355.1 9.4 %copy-start.7 = (f32[256,1024]{0,1:T(8,128)S(1)}, f32[256,1024]{0,1:T(8,128)}, u32[]{:S(2)}) copy-start(f32[256,1024]{0,1:T(8,128)} %get-tuple-element.31) | copy-start | bytes 3145732
  444.0 2.0 copy-start.1
  494.2 2.0 copy-start
Sparse Core Ops, SparseCore 0:
  13.8 280.3 all-reduce.5
  382.8 51.2 all-reduce.7
where the time goes:
time: 834 us; the launch traced here: 822 us
  waiting for transfers between devices  333 us (40%)
  other arithmetic  265 us (32%)
  matrix products  144 us (17%)
  local copies, waits for them, and re-layouts  60.1 us (7%)
  between operations  19.2 us (2%)
    psum x1, waiting for transfers between devices, spread(): return lax.psum(block, axis)  282 us
    another operation x31, other arithmetic, shards(): diag_factor = jnp.linalg.cholesky(diag_block)  169 us
    another operation x3, other arithmetic, shards(): jax.scipy.linalg.solve_triangular(diag_factor, flat_reduced.T, lower=True)  83.9 us
    dot_general x1, matrix products, shards(): jnp.dot(flat_rows, target.T, precision=lax.Precision.HIGHEST, preferred_e...  55.7 us
    psum x1, waiting for transfers between devices, shards(): whole = lax.psum(product.reshape(cycle_count, row_block, width), 'layers')  51.3 us
    another operation x15, matrix products, shards(): jax.scipy.linalg.solve_triangular(diag_factor, flat_reduced.T, lower=True)  44 us
    another operation x14, matrix products, shards(): diag_factor = jnp.linalg.cholesky(diag_block)  26.2 us
    another operation x40, local copies, waits for them, and re-layouts  23.1 us
  transfers between devices with their start and end apart: 2, of which 2 were waited for; matrix products, arithmetic and copies ran while one was open for 0% of the time, Pallas kernels for 0%

commit v1 on v0

v1 whole, which is shorter than its diff:
```python
import functools
import jax
import jax.numpy as jnp
from jax import lax
from jax.experimental import pallas as pl
from jax.experimental.pallas import tpu as pltpu
from jax.sharding import PartitionSpec as P

MESH = pl.DeviceIdType.MESH
HIGH = lax.Precision.HIGH
TILE = 128
CHUNKS = 4


def gather_kernel(groups, peers, f_ref, p_ref, t_ref, d_ref, local_sem, z_send, z_recv, g_send, g_recv):
    row = lax.axis_index("rows")
    layer = lax.axis_index("layers")
    group = row // peers
    place = lax.rem(row, peers)
    base = group * peers
    has_prev = group > 0
    has_next = group < groups - 1
    prev = jnp.where(has_prev, row - peers, row)
    following = jnp.where(has_next, row + peers, row)
    size = f_ref.shape[0]
    part = size // CHUNKS

    barrier = pltpu.get_barrier_semaphore()

    def greet(who):
        pl.semaphore_signal(barrier, inc=1, device_id=(who, layer), device_id_type=MESH)

    for k in range(1, peers):
        greet(base + lax.rem(place + k, peers))

    @pl.when(has_prev)
    def _():
        greet(prev)

    @pl.when(has_next)
    def _():
        greet(following)

    pl.semaphore_wait(barrier, peers - 1 + has_prev.astype(jnp.int32) + has_next.astype(jnp.int32))

    def rows_of(owner, c):
        return pl.ds(pl.multiple_of(owner * size + c * part, part), part)

    def chain(a, dst, c):
        return pltpu.make_async_remote_copy(
            src_ref=dst.at[rows_of(place, c)], dst_ref=dst.at[rows_of(place, c)],
            send_sem=z_send.at[a, c], recv_sem=z_recv.at[a, c],
            device_id=(following, layer), device_id_type=MESH)

    def spread(a, dst, c, k):
        to = base + lax.rem(place + k, peers)
        return pltpu.make_async_remote_copy(
            src_ref=dst.at[rows_of(place, c)], dst_ref=dst.at[rows_of(place, c)],
            send_sem=g_send.at[a, c, k], recv_sem=g_recv.at[a, c, k],
            device_id=(to, layer), device_id_type=MESH)

    def arrival(a, dst, c, k):
        src = lax.rem(place + peers - k, peers)
        return pltpu.make_async_remote_copy(
            src_ref=dst.at[rows_of(src, c)], dst_ref=dst.at[rows_of(src, c)],
            send_sem=g_send.at[a, c, k], recv_sem=g_recv.at[a, c, k],
            device_id=(base + src, layer), device_id_type=MESH)

    def each(body):
        body(0, f_ref, t_ref)

        @pl.when(layer == 0)
        def _():
            body(1, p_ref, d_ref)

    def own(a, src, dst):
        return pltpu.make_async_copy(src, dst.at[pl.ds(pl.multiple_of(place * size, size), size)], local_sem.at[a])

    @pl.when(jnp.logical_not(has_prev))
    def _():
        each(lambda a, src, dst: own(a, src, dst).start())
        each(lambda a, src, dst: own(a, src, dst).wait())

    for c in range(CHUNKS):
        def step(a, src, dst):
            @pl.when(has_prev)
            def _():
                chain(a, dst, c).wait_recv()

            @pl.when(has_next)
            def _():
                chain(a, dst, c).start()

            for k in range(1, peers):
                spread(a, dst, c, k).start()

        each(step)

    for c in range(CHUNKS):
        def finish(a, src, dst):
            for k in range(1, peers):
                arrival(a, dst, c, k).wait_recv()
                spread(a, dst, c, k).wait_send()

            @pl.when(has_next)
            def _():
                chain(a, dst, c).wait_send()

        each(finish)


def gather(groups, peers, f, p):
    rows, cols = f.shape
    out = jax.ShapeDtypeStruct((peers * rows, cols), f.dtype)
    out_p = jax.ShapeDtypeStruct((peers * rows, p.shape[1]), p.dtype)
    dma = pltpu.SemaphoreType.DMA
    return pl.pallas_call(
        functools.partial(gather_kernel, groups, peers),
        out_shape=(out, out_p),
        in_specs=[pl.BlockSpec(memory_space=pl.ANY)] * 2,
        out_specs=(pl.BlockSpec(memory_space=pl.ANY),) * 2,
        scratch_shapes=[dma((2,)), dma((2, CHUNKS)), dma((2, CHUNKS)),
                        dma((2, CHUNKS, peers)), dma((2, CHUNKS, peers))],
        compiler_params=pltpu.CompilerParams(collective_id=0, has_side_effects=True),
    )(f, p)


def split(x):
    hi = x.astype(jnp.bfloat16)
    return hi, (x - hi.astype(jnp.float32)).astype(jnp.bfloat16)


def dot3(a, b):
    a_hi, a_lo = a
    b_hi, b_lo = b
    mm = functools.partial(jnp.dot, preferred_element_type=jnp.float32)
    return mm(a_hi, b_hi) + (mm(a_hi, b_lo) + mm(a_lo, b_hi))


def base_inverse(block):
    n = TILE // 8
    sub = lax.broadcasted_iota(jnp.int32, (8, TILE), 0)
    lane = lax.broadcasted_iota(jnp.int32, (8, TILE), 1)
    a = [block[8 * i:8 * i + 8, :] for i in range(n)]
    x = [jnp.where(lane == sub + 8 * i, 1.0, 0.0).astype(jnp.float32) for i in range(n)]
    for j in range(TILE):
        s, o = j // 8, j % 8
        row = jnp.broadcast_to(a[s][o:o + 1, :], (8, TILE))
        root = lax.rsqrt(jnp.broadcast_to(row[:, j:j + 1], (8, TILE)))
        row = row * root
        xrow = jnp.broadcast_to(x[s][o:o + 1, :], (8, TILE)) * root
        for i in range(s, n):
            col = jnp.broadcast_to(a[i][:, j:j + 1], (8, TILE)) * root
            if i == s:
                x[i] = jnp.where(sub == o, xrow, jnp.where(sub > o, x[i] - col * xrow, x[i]))
                a[i] = a[i] - jnp.where(sub > o, col, 0.0) * row
            else:
                a[i] = a[i] - col * row
                x[i] = x[i] - col * xrow
    return jnp.concatenate(x, 0)


def inverse_kernel(d_ref, o_ref, m_ref):
    size = d_ref.shape[0]
    count = size // TILE
    m_ref[...] = d_ref[...]
    col_tile = lax.broadcasted_iota(jnp.int32, (TILE, size), 1) // TILE
    eye = (lax.broadcasted_iota(jnp.int32, (TILE, TILE), 0)
           == lax.broadcasted_iota(jnp.int32, (TILE, TILE), 1)).astype(jnp.float32)

    @pl.loop(0, count)
    def _(b):
        here = pl.ds(pl.multiple_of(b * TILE, TILE), TILE)
        inv = base_inverse(m_ref[here, here])
        m_ref[here, here] = eye
        u = dot3(split(inv), split(m_ref[here, :]))
        o_ref[here, :] = jnp.where(col_tile <= b, u, 0.0)
        m_ref[here, :] = u
        u_parts = split(u)

        @pl.loop(b + 1, count)
        def _(i):
            there = pl.ds(pl.multiple_of(i * TILE, TILE), TILE)
            left = m_ref[here, there].T
            old = jnp.where(col_tile == b, 0.0, m_ref[there, :])
            m_ref[there, :] = old - dot3(split(left), u_parts)


def factor_inverse(d):
    size = d.shape[0]
    return pl.pallas_call(
        inverse_kernel,
        out_shape=jax.ShapeDtypeStruct((size, size), jnp.float32),
        in_specs=[pl.BlockSpec(memory_space=pltpu.VMEM)],
        out_specs=pl.BlockSpec(memory_space=pltpu.VMEM),
        scratch_shapes=[pltpu.VMEM((size, size), jnp.float32)],
        compiler_params=pltpu.CompilerParams(vmem_limit_bytes=32 * 1024 * 1024),
        cost_estimate=pl.CostEstimate(flops=size ** 3 * 60, bytes_accessed=8 * size * size, transcendentals=0),
    )(d)


def dot_t(a, b):
    return lax.dot_general(a, b, (((1,), (1,)), ((), ())), precision=HIGH, preferred_element_type=jnp.float32)


def shards(rows_count, panel, factor):
    own_cycles, row_block, width = panel.shape
    peers = width // row_block
    layer = lax.axis_index("layers")
    swap = [(0, 1), (1, 0)]
    target, diag_input = gather(rows_count // peers, peers, factor[0], panel[0])
    square = jnp.where(layer == 0, diag_input, 0.0) - dot_t(target, target)
    diag_block = square + lax.ppermute(square, "layers", swap)
    flat = factor.reshape(2, own_cycles * row_block, factor.shape[2])
    other = dot_t(lax.dynamic_index_in_dim(flat, 1 - layer, 0, False), target)
    from_other = lax.ppermute(other, "layers", swap)
    mine = dot_t(lax.dynamic_index_in_dim(flat, layer, 0, False), target)
    inverse = factor_inverse(diag_block)
    reduced = panel.reshape(-1, width) - (mine + from_other)
    return dot_t(reduced, inverse).reshape(panel.shape)


def solution(mesh):
    in_specs = (P("layers", "rows", None), P(None, "rows", "layers"))
    out_specs = P("layers", "rows", None)
    body = functools.partial(shards, mesh.shape["rows"])
    return jax.shard_map(body, mesh=mesh, in_specs=in_specs, out_specs=out_specs, check_vma=False)
```

time: 834 us -> 333 us (0.40); the launches traced: 822 us -> 333 us
  waiting for transfers between devices: 333 us -> 0.01 us
  other arithmetic: 265 us -> 4.55 us
  Pallas kernels: 0 us -> 224 us
  matrix products: 144 us -> 41.2 us
  starting transfers between devices: 0.04 us -> 60 us
  local copies, waits for them, and re-layouts: 60.1 us -> 3.21 us
  between operations: 19.2 us -> 0.11 us
    psum x2 -> x0, waiting for transfers between devices: 333 us -> none  [the longest x1 282 us: spread(): return lax.psum(block, axis)]
    another operation x34 -> x0, other arithmetic: 253 us -> none  [the longest x31 169 us: shards(): diag_factor = jnp.linalg.cholesky(diag_block)]
    pallas_call x0 -> x2, Pallas kernels: none -> 224 us  [the longest x1 151 us: factor_inverse(): pl.pallas_call(inverse_kernel, out_shape=jax.ShapeDtypeStruct((size, size...]
    another operation x29 -> x0, matrix products: 70.2 us -> none  [the longest x15 44 us: shards(): jax.scipy.linalg.solve_triangular(diag_factor, flat_reduced.T, lower=True)]
    ppermute x0 -> x2, starting transfers between devices: none -> 60 us  [the longest x1 60 us: shards(): diag_block = square + lax.ppermute(square, 'layers', swap)]
    dot_general x2 -> x4, matrix products: 73.8 us -> 41.2 us  [dot_t(): lax.dot_general(a, b, (((1,), (1,)), ((), ())), precision=HIGH, preferred...]
    another operation x66 -> x0, local copies, waits for them, and re-layouts: 28.5 us -> none
    reshape x2 -> x0, local copies, waits for them, and re-layouts: 14.8 us -> none  [the longest x1 9.43 us: shards(): whole = lax.psum(product.reshape(cycle_count, row_block, width), 'layers')]
  transfers between devices with their start and end apart: 2 -> 2, of which waited for: 2 -> 0; matrix products, arithmetic and copies ran while one was open for 0% -> 5% of each run, Pallas kernels for 0% -> 45%
where the time goes in v1:
time: 333 us
  Pallas kernels  224 us (67%)
  starting transfers between devices  60 us (18%)
  matrix products  41.2 us (12%)
  other arithmetic  4.55 us (1%)
    pallas_call x1, Pallas kernels, factor_inverse(): pl.pallas_call(inverse_kernel, out_shape=jax.ShapeDtypeStruct((size, size...  151 us
    pallas_call x1, Pallas kernels, gather(): pl.pallas_call(functools.partial(gather_kernel, groups, peers), out_shape...  72.7 us
    ppermute x1, starting transfers between devices, shards(): diag_block = square + lax.ppermute(square, 'layers', swap)  60 us
    dot_general x4, matrix products, dot_t(): lax.dot_general(a, b, (((1,), (1,)), ((), ())), precision=HIGH, preferred...  41.2 us
  transfers between devices with their start and end apart: 2, of which 0 were waited for; matrix products, arithmetic and copies ran while one was open for 5% of the time, Pallas kernels for 45%

profile of v1, /device:TPU:25, one launch (start us, length us, event | category | flops | bytes accessed | tf_op | source)
XLA Modules:
  0.0 332.8 jit_solution(7268605210046542034)
XLA Ops:
  0.0 3.2 slice_bitcast_fusion
  3.2 72.7 %shard_map.28 = (f32[1024,1024]{1,0:T(8,128)}, f32[1024,1024]{1,0:T(8,128)}) custom-call(f32[256,1024]{1,0:T(8,128)} %get-tuple-element.10.f_ref, f32[256,1024]{1,0:T(8,128)} %get-tuple-element.9.p_ref), custom_call_target="tpu_custom_call" | custom-call | tf_op jit(solution)/shard_map/pallas_call | solution.py:117
  75.9 11.7 %select_subtract_fusion = f32[1024,1024]{1,0:T(8,128)} fusion(f32[1024,1024]{1,0:T(8,128)} %get-tuple-element.8, pred[]{:T(512)S(6)} %eq.3, f32[1024,1024]{1,0:T(8,128)} %get-tuple-element.7), kind=kOutput, calls=%fused_computation.5 | convolution fusion | flops 6444548096 | bytes 12582913 | tf_op jit(solution)/shard_map/dot_general | solution.py:203
  87.6 60.0 %collective-permute-start.1 = (f32[1024,1024]{1,0:T(8,128)}, f32[1024,1024]{1,0:T(8,128)}, u32[]{:S(2)}, u32[]{:S(2)}) collective-permute-start(f32[1024,1024]{1,0:T(8,128)} %select_subtract_fusion), channel_id=1, source_target_pairs={{0,1},{1,0},{2,3},{3,2},{4,5},{5,4},{6,7},{7,6},{8,9},{9,8},{10,11... | collective-permute-start | bytes 12582920 | tf_op jit(solution)/shard_map/ppermute | solution.py:213
  147.6 11.1 %fusion = f32[1024,1024]{1,0:T(8,128)} fusion(f32[1024,1024]{1,0:T(8,128)} %get-tuple-element.7, f32[2,1024,1024]{2,1,0:T(8,128)} %bitcast.22, s32[]{:T(128)S(6)} %select_n.16), kind=kOutput, calls=%fused_computation | convolution fusion | flops 6442450944 | bytes 12582916 | tf_op jit(solution)/shard_map/dot_general | solution.py:203
  158.7 0.0 collective-permute-start
  158.8 0.0 collective-permute-done.1
  158.8 0.0 slice-start
  158.8 4.5 %add.17.d_ref = f32[1024,1024]{1,0:T(8,128)S(1)} add(f32[1024,1024]{1,0:T(8,128)} %select_subtract_fusion, f32[1024,1024]{1,0:T(8,128)} %collective-permute-done.1) | non-fusion elementwise | flops 1048576 | bytes 12582912 | tf_op jit(solution)/shard_map/add | solution.py:213
  163.3 0.0 copy-start
  163.3 0.0 copy-start.1
  163.4 0.0 slice-start.1
  163.4 150.9 %shard_map.29 = f32[1024,1024]{1,0:T(8,128)S(1)} custom-call(f32[1024,1024]{1,0:T(8,128)S(1)} %add.17.d_ref), custom_call_target="tpu_custom_call" | custom-call | flops 64424509440 | bytes 8388608 | tf_op jit(solution)/shard_map/pallas_call | solution.py:191
  314.3 0.0 collective-permute-done
  314.3 0.0 slice-done
  314.3 0.0 copy-done
  314.3 0.0 copy-done.1
  314.4 0.0 slice-done.1
  314.4 10.0 %bitcast_subtract_fusion = f32[1024,1024]{1,0:T(8,128)S(1)} fusion(f32[4,256,1024]{2,1,0:T(8,128)S(1)} %copy-done.1, f32[1024,1024]{1,0:T(8,128)} %collective-permute-done, f32[1024,1024]{1,0:T(8,128)S(1)} %copy-done, f32[2,1024,1024]{2,1,0:T(8,128)S(1)} %bitcast.25, s32[]{:T(128)S(6)} %select_n.15), kind=kOutput, calls=%fused_computation.4 | convolution fusion | flops 6444548096 | bytes 20971524 | tf_op jit(solution)/shard_map/dot_general | solution.py:203
  324.4 8.3 %fusion.10 = f32[1024,1024]{1,0:T(8,128)} fusion(f32[1024,1024]{1,0:T(8,128)S(1)} %bitcast_subtract_fusion, f32[1024,1024]{1,0:T(8,128)S(1)} %shard_map.29), kind=kOutput, calls=%fused_computation.12 | convolution fusion | flops 6442450944 | bytes 12582912 | tf_op jit(solution)/shard_map/dot_general | solution.py:203
  (1 shorter events, 0.0 us)
Async XLA Ops:
  87.6 71.1 %collective-permute-start.1 = (f32[1024,1024]{1,0:T(8,128)}, f32[1024,1024]{1,0:T(8,128)}, u32[]{:S(2)}, u32[]{:S(2)}) collective-permute-start(f32[1024,1024]{1,0:T(8,128)} %select_subtract_fusion), channel_id=1, source_target_pairs={{0,1},{1,0},{2,3},{3,2},{4,5},{5,4},{6,7},{7,6},{8,9},{9,8},{10,11... | collective-permute-start | bytes 12582920 | tf_op jit(solution)/shard_map/ppermute | solution.py:213
  158.7 155.6 %collective-permute-start = (f32[1024,1024]{1,0:T(8,128)}, f32[1024,1024]{1,0:T(8,128)}, u32[]{:S(2)}, u32[]{:S(2)}) collective-permute-start(f32[1024,1024]{1,0:T(8,128)} %fusion), channel_id=1, source_target_pairs={{0,1},{1,0},{2,3},{3,2},{4,5},{5,4},{6,7},{7,6},{8,9},{9,8},{10,11... | collective-permute-start | bytes 12582920 | tf_op jit(solution)/shard_map/ppermute | solution.py:216
  158.8 155.6 %slice-start = ((s8[8388608]{0:T(1024)(128)(4,1)}), s8[4194304]{0:T(1024)(128)(4,1)S(1)}, s32[]{:S(2)}) async-start(s8[8388608]{0:T(1024)(128)(4,1)} %bitcast.23), calls=%async_computation | async-start | bytes 8388608
  163.3 151.0 %copy-start = (f32[1024,1024]{1,0:T(8,128)S(1)}, f32[1024,1024]{1,0:T(8,128)}, u32[]{:S(2)}) copy-start(f32[1024,1024]{1,0:T(8,128)} %get-tuple-element.7) | copy-start | bytes 12582916
  163.3 151.0 %copy-start.1 = (f32[4,256,1024]{2,1,0:T(8,128)S(1)}, f32[4,256,1024]{2,1,0:T(8,128)}, u32[]{:S(2)}) copy-start(f32[4,256,1024]{2,1,0:T(8,128)} %param.2) | copy-start | bytes 12582916
  163.4 151.0 %slice-start.1 = ((s8[8388608]{0:T(1024)(128)(4,1)}), s8[4194304]{0:T(1024)(128)(4,1)S(1)}, s32[]{:S(2)}) async-start(s8[8388608]{0:T(1024)(128)(4,1)} %bitcast.23), calls=%async_computation.1 | async-start | bytes 8388608

commit v2 on v1

--- a/solution.py
+++ b/solution.py
@@ -22,8 +22,9 @@
     has_next = group < groups - 1
     prev = jnp.where(has_prev, row - peers, row)
     following = jnp.where(has_next, row + peers, row)
-    size = f_ref.shape[0]
-    part = size // CHUNKS
+    heights = (f_ref.shape[0], p_ref.shape[0])
+    part = heights[0] // CHUNKS
+    wide = p_ref.shape[1] // peers
 
     barrier = pltpu.get_barrier_semaphore()
 
@@ -43,46 +44,54 @@
 
     pl.semaphore_wait(barrier, peers - 1 + has_prev.astype(jnp.int32) + has_next.astype(jnp.int32))
 
-    def rows_of(owner, c):
-        return pl.ds(pl.multiple_of(owner * size + c * part, part), part)
+    def piece(a, dst, owner, c):
+        if a == 0:
+            return dst.at[pl.ds(pl.multiple_of(owner * heights[0] + c * part, part), part)]
+        return dst.at[pl.ds(pl.multiple_of(owner * heights[1], heights[1]), heights[1]), pl.ds(c * wide, wide)]
 
     def chain(a, dst, c):
         return pltpu.make_async_remote_copy(
-            src_ref=dst.at[rows_of(place, c)], dst_ref=dst.at[rows_of(place, c)],
+            src_ref=piece(a, dst, place, c), dst_ref=piece(a, dst, place, c),
             send_sem=z_send.at[a, c], recv_sem=z_recv.at[a, c],
             device_id=(following, layer), device_id_type=MESH)
 
     def spread(a, dst, c, k):
         to = base + lax.rem(place + k, peers)
         return pltpu.make_async_remote_copy(
-            src_ref=dst.at[rows_of(place, c)], dst_ref=dst.at[rows_of(place, c)],
+            src_ref=piece(a, dst, place, c), dst_ref=piece(a, dst, place, c),
             send_sem=g_send.at[a, c, k], recv_sem=g_recv.at[a, c, k],
             device_id=(to, layer), device_id_type=MESH)
 
     def arrival(a, dst, c, k):
         src = lax.rem(place + peers - k, peers)
         return pltpu.make_async_remote_copy(
-            src_ref=dst.at[rows_of(src, c)], dst_ref=dst.at[rows_of(src, c)],
+            src_ref=piece(a, dst, src, c), dst_ref=piece(a, dst, src, c),
             send_sem=g_send.at[a, c, k], recv_sem=g_recv.at[a, c, k],
             device_id=(base + src, layer), device_id_type=MESH)
 
-    def each(body):
-        body(0, f_ref, t_ref)
-
-        @pl.when(layer == 0)
-        def _():
-            body(1, p_ref, d_ref)
+    work = ((0, f_ref, t_ref), (1, p_ref, d_ref))
+    steps = [(a, dst, c) for c in range(max(CHUNKS, peers))
+             for a, dst in ((0, t_ref), (1, d_ref)) if c < (CHUNKS, peers)[a]]
+
+    def when_used(a, owner, c, body):
+        if a == 0:
+            body()
+        else:
+            pl.when(c >= owner)(body)
 
     def own(a, src, dst):
-        return pltpu.make_async_copy(src, dst.at[pl.ds(pl.multiple_of(place * size, size), size)], local_sem.at[a])
+        start = pl.multiple_of(place * heights[a], heights[a])
+        return pltpu.make_async_copy(src, dst.at[pl.ds(start, heights[a])], local_sem.at[a])
 
     @pl.when(jnp.logical_not(has_prev))
     def _():
-        each(lambda a, src, dst: own(a, src, dst).start())
-        each(lambda a, src, dst: own(a, src, dst).wait())
-
-    for c in range(CHUNKS):
-        def step(a, src, dst):
+        for item in work:
+            own(*item).start()
+        for item in work:
+            own(*item).wait()
+
+    for a, dst, c in steps:
+        def step(a=a, dst=dst, c=c):
             @pl.when(has_prev)
             def _():
                 chain(a, dst, c).wait_recv()
@@ -94,33 +103,36 @@
             for k in range(1, peers):
                 spread(a, dst, c, k).start()
 
-        each(step)
-
-    for c in range(CHUNKS):
-        def finish(a, src, dst):
+        when_used(a, place, c, step)
+
+    for a, dst, c in steps:
+        def finish(a=a, dst=dst, c=c):
             for k in range(1, peers):
-                arrival(a, dst, c, k).wait_recv()
                 spread(a, dst, c, k).wait_send()
 
             @pl.when(has_next)
             def _():
                 chain(a, dst, c).wait_send()
 
-        each(finish)
+        when_used(a, place, c, finish)
+        for k in range(1, peers):
+            src = lax.rem(place + peers - k, peers)
+            when_used(a, src, c, lambda a=a, dst=dst, c=c, k=k: arrival(a, dst, c, k).wait_recv())
 
 
 def gather(groups, peers, f, p):
     rows, cols = f.shape
     out = jax.ShapeDtypeStruct((peers * rows, cols), f.dtype)
-    out_p = jax.ShapeDtypeStruct((peers * rows, p.shape[1]), p.dtype)
+    out_p = jax.ShapeDtypeStruct((peers * p.shape[0], p.shape[1]), p.dtype)
+    count = max(CHUNKS, peers)
     dma = pltpu.SemaphoreType.DMA
     return pl.pallas_call(
         functools.partial(gather_kernel, groups, peers),
         out_shape=(out, out_p),
         in_specs=[pl.BlockSpec(memory_space=pl.ANY)] * 2,
         out_specs=(pl.BlockSpec(memory_space=pl.ANY),) * 2,
-        scratch_shapes=[dma((2,)), dma((2, CHUNKS)), dma((2, CHUNKS)),
-                        dma((2, CHUNKS, peers)), dma((2, CHUNKS, peers))],
+        scratch_shapes=[dma((2,)), dma((2, count)), dma((2, count)),
+                        dma((2, count, peers)), dma((2, count, peers))],
         compiler_params=pltpu.CompilerParams(collective_id=0, has_side_effects=True),
     )(f, p)
 
@@ -137,26 +149,71 @@
     return mm(a_hi, b_hi) + (mm(a_hi, b_lo) + mm(a_lo, b_hi))
 
 
+def small_inverse(e):
+    low = [[None] * 8 for _ in range(8)]
+    inv = [[None] * 8 for _ in range(8)]
+    for j in range(8):
+        root = lax.rsqrt(e[j][j])
+        inv[j][j] = root
+        for k in range(j):
+            total = low[j][k] * inv[k][k]
+            for m in range(k + 1, j):
+                total = total + low[j][m] * inv[m][k]
+            inv[j][k] = -(root * total)
+        for i in range(j + 1, 8):
+            low[i][j] = e[i][j] * root
+        for i in range(j + 1, 8):
+            for k in range(j + 1, i + 1):
+                e[i][k] = e[i][k] - low[i][j] * low[k][j]
+    return inv
+
+
+def spread_row(tile, k):
+    return jnp.broadcast_to(tile[k:k + 1, :], (8, TILE))
+
+
+def combine(columns, tiles):
+    total = columns[0] * tiles[0]
+    for k in range(1, 8):
+        total = total + columns[k] * tiles[k]
+    return total
+
+
 def base_inverse(block):
     n = TILE // 8
     sub = lax.broadcasted_iota(jnp.int32, (8, TILE), 0)
     lane = lax.broadcasted_iota(jnp.int32, (8, TILE), 1)
+    is_row = [sub == k for k in range(8)]
+    zero = jnp.zeros((8, TILE), jnp.float32)
     a = [block[8 * i:8 * i + 8, :] for i in range(n)]
     x = [jnp.where(lane == sub + 8 * i, 1.0, 0.0).astype(jnp.float32) for i in range(n)]
-    for j in range(TILE):
-        s, o = j // 8, j % 8
-        row = jnp.broadcast_to(a[s][o:o + 1, :], (8, TILE))
-        root = lax.rsqrt(jnp.broadcast_to(row[:, j:j + 1], (8, TILE)))
-        row = row * root
-        xrow = jnp.broadcast_to(x[s][o:o + 1, :], (8, TILE)) * root
-        for i in range(s, n):
-            col = jnp.broadcast_to(a[i][:, j:j + 1], (8, TILE)) * root
-            if i == s:
-                x[i] = jnp.where(sub == o, xrow, jnp.where(sub > o, x[i] - col * xrow, x[i]))
-                a[i] = a[i] - jnp.where(sub > o, col, 0.0) * row
-            else:
-                a[i] = a[i] - col * row
-                x[i] = x[i] - col * xrow
+    for s in range(n):
+        head = a[s]
+        e = [[jnp.broadcast_to(head[i:i + 1, 8 * s + k:8 * s + k + 1], (8, TILE)) for k in range(i + 1)]
+             for i in range(8)]
+        inv = small_inverse(e)
+        columns, rows = [], []
+        for k in range(8):
+            column, row = zero, zero
+            for i in range(k, 8):
+                column = jnp.where(is_row[i], inv[i][k], column)
+            for i in range(k + 1):
+                row = jnp.where(is_row[i], inv[k][i], row)
+            columns.append(column)
+            rows.append(row)
+        xs = combine(columns, [spread_row(x[s], k) for k in range(8)])
+        x[s] = xs
+        if s == n - 1:
+            break
+        us = combine(columns, [spread_row(head, k) for k in range(8)])
+        wa = combine(rows, [spread_row(us, k) for k in range(8)])
+        wx = combine(rows, [spread_row(xs, k) for k in range(8)])
+        wa = [spread_row(wa, k) for k in range(8)]
+        wx = [spread_row(wx, k) for k in range(8)]
+        for i in range(s + 1, n):
+            cols = [jnp.broadcast_to(a[i][:, 8 * s + k:8 * s + k + 1], (8, TILE)) for k in range(8)]
+            a[i] = a[i] - combine(cols, wa)
+            x[i] = x[i] - combine(cols, wx)
     return jnp.concatenate(x, 0)
 
 
@@ -208,8 +265,13 @@
     peers = width // row_block
     layer = lax.axis_index("layers")
     swap = [(0, 1), (1, 0)]
-    target, diag_input = gather(rows_count // peers, peers, factor[0], panel[0])
-    square = jnp.where(layer == 0, diag_input, 0.0) - dot_t(target, target)
+    half = row_block // 2
+    second = lax.ppermute(panel[0, half:], "layers", [(0, 1)])
+    share = jnp.where(layer == 0, panel[0, :half], second)
+    target, diag_share = gather(rows_count // peers, peers, factor[0], share)
+    slot = lax.broadcasted_iota(jnp.int32, (1, 2, 1, 1), 1) == layer
+    diag_input = jnp.where(slot, diag_share.reshape(peers, 1, half, width), 0.0).reshape(width, width)
+    square = diag_input - dot_t(target, target)
     diag_block = square + lax.ppermute(square, "layers", swap)
     flat = factor.reshape(2, own_cycles * row_block, factor.shape[2])
     other = dot_t(lax.dynamic_index_in_dim(flat, 1 - layer, 0, False), target)

time: 333 us -> 244 us (0.73)
  starting transfers between devices: 60 us -> 7.81 us
  Pallas kernels: 224 us -> 184 us
    pallas_call x1, Pallas kernels: 151 us -> 56.4 us  [factor_inverse(): pl.pallas_call(inverse_kernel, out_shape=jax.ShapeDtypeStruct((size, size...]
    pallas_call x1, Pallas kernels: 72.7 us -> 128 us  [gather(): pl.pallas_call(functools.partial(gather_kernel, groups, peers), out_shape...]
    ppermute x1, starting transfers between devices: 60 us -> 6.45 us  [shards(): diag_block = square + lax.ppermute(square, 'layers', swap)]
  transfers between devices with their start and end apart: 2 -> 3, of which waited for: 0 -> 1; matrix products, arithmetic and copies ran while one was open for 5% -> 7% of each run, Pallas kernels for 45% -> 23%
where the time goes in v2:
time: 244 us; the launch traced here: 243 us
  Pallas kernels  184 us (75%)
  matrix products  40.5 us (17%)
  starting transfers between devices  7.81 us (3%)
  other arithmetic  6.31 us (3%)
  local copies, waits for them, and re-layouts  3.49 us (1%)
    pallas_call x1, Pallas kernels, gather(): pl.pallas_call(functools.partial(gather_kernel, groups, peers), out_shape...  128 us
    pallas_call x1, Pallas kernels, factor_inverse(): pl.pallas_call(inverse_kernel, out_shape=jax.ShapeDtypeStruct((size, size...  56.4 us
    dot_general x4, matrix products, dot_t(): lax.dot_general(a, b, (((1,), (1,)), ((), ())), precision=HIGH, preferred...  40.5 us
    ppermute x1, starting transfers between devices, shards(): diag_block = square + lax.ppermute(square, 'layers', swap)  6.45 us
  transfers between devices with their start and end apart: 3, of which 1 were waited for; matrix products, arithmetic and copies ran while one was open for 7% of the time, Pallas kernels for 23%

profile of v2, /device:TPU:25, one launch (start us, length us, event | category | flops | bytes accessed | tf_op | source)
XLA Modules:
  0.0 242.8 jit_solution(4636885887770747411)
XLA Ops:
  0.0 1.1 slice_bitcast_fusion.1
  1.1 1.3 collective-permute-start
  2.4 0.1 broadcast_in_dim.28
  2.5 2.3 slice_bitcast_fusion.f_ref
  4.8 0.1 collective-permute-done
  4.9 1.9 bitcast_select_fusion.1.p_ref
  6.8 128.1 %shard_map.28 = (f32[1024,1024]{1,0:T(8,128)}, f32[512,1024]{1,0:T(8,128)}) custom-call(f32[256,1024]{1,0:T(8,128)} %slice_bitcast_fusion.f_ref, f32[128,1024]{1,0:T(8,128)} %bitcast_select_fusion.1.p_ref), custom_call_target="tpu_custom_call" | custom-call | tf_op jit(solution)/shard_map/pallas_call | solution.py:129
  134.9 12.3 %fusion = f32[1024,1024]{1,0:T(8,128)} fusion(f32[4,128,1024]{2,1,0:T(8,128)} %bitcast.31, pred[1024]{0:T(1024)(128)(4,1)S(1)} %broadcast_in_dim.29, f32[1024,1024]{1,0:T(8,128)} %get-tuple-element.7), kind=kOutput, calls=%fused_computation.1 | convolution fusion | flops 6444548096 | bytes 10486784 | tf_op jit(solution)/shard_map/dot_general | solution.py:260
  147.1 6.4 %collective-permute-start.2 = (f32[1024,1024]{1,0:T(8,128)}, f32[1024,1024]{1,0:T(8,128)}, u32[]{:S(2)}, u32[]{:S(2)}) collective-permute-start(f32[1024,1024]{1,0:T(8,128)} %fusion), channel_id=1, source_target_pairs={{0,1},{1,0},{2,3},{3,2},{4,5},{5,4},{6,7},{7,6},{8,9},{9,8},{10,11... | collective-permute-start | bytes 12582920 | tf_op jit(solution)/shard_map/ppermute | solution.py:275
  153.6 10.5 %fusion.1 = f32[1024,1024]{1,0:T(8,128)S(1)} fusion(f32[1024,1024]{1,0:T(8,128)} %get-tuple-element.7, f32[2,1024,1024]{2,1,0:T(8,128)} %bitcast.29, s32[]{:T(128)S(6)} %select_n.23), kind=kOutput, calls=%fused_computation.2 | convolution fusion | flops 6442450944 | bytes 12582916 | tf_op jit(solution)/shard_map/dot_general | solution.py:260
  164.1 0.1 collective-permute-start.1
  164.2 0.0 collective-permute-done.2
  164.2 4.4 %add.17.d_ref = f32[1024,1024]{1,0:T(8,128)S(1)} add(f32[1024,1024]{1,0:T(8,128)} %fusion, f32[1024,1024]{1,0:T(8,128)} %collective-permute-done.2) | non-fusion elementwise | flops 1048576 | bytes 12582912 | tf_op jit(solution)/shard_map/add | solution.py:275
  168.6 0.0 copy-start
  168.6 0.0 copy-start.1
  168.6 56.4 %shard_map.29 = f32[1024,1024]{1,0:T(8,128)S(1)} custom-call(f32[1024,1024]{1,0:T(8,128)S(1)} %add.17.d_ref), custom_call_target="tpu_custom_call" | custom-call | flops 64424509440 | bytes 8388608 | tf_op jit(solution)/shard_map/pallas_call | solution.py:248
  225.0 0.0 collective-permute-done.1
  225.0 0.0 copy-done
  225.0 0.0 copy-done.1
  225.0 9.4 %bitcast_subtract_fusion = f32[1024,1024]{1,0:T(8,128)S(1)} fusion(f32[4,256,1024]{2,1,0:T(8,128)S(1)} %copy-done.1, f32[1024,1024]{1,0:T(8,128)S(1)} %collective-permute-done.1, f32[1024,1024]{1,0:T(8,128)S(1)} %copy-done, f32[2,1024,1024]{2,1,0:T(8,128)} %bitcast.30, s32[]{:T(128)S(6)} %select_n.20), kind=kOutput, calls=%fused_computation.6 | convolution fusion | flops 6444548096 | bytes 20971524 | tf_op jit(solution)/shard_map/dot_general | solution.py:260
  234.4 8.3 %fusion.11 = f32[1024,1024]{1,0:T(8,128)} fusion(f32[1024,1024]{1,0:T(8,128)S(1)} %bitcast_subtract_fusion, f32[1024,1024]{1,0:T(8,128)S(1)} %shard_map.29), kind=kOutput, calls=%fused_computation.15 | convolution fusion | flops 6442450944 | bytes 12582912 | tf_op jit(solution)/shard_map/dot_general | solution.py:260
  (2 shorter events, 0.0 us)
Async XLA Ops:
  1.1 3.8 %collective-permute-start = (f32[128,1024]{1,0:T(8,128)S(1)}, f32[128,1024]{1,0:T(8,128)S(1)}, u32[]{:S(2)}, u32[]{:S(2)}) collective-permute-start(f32[128,1024]{1,0:T(8,128)S(1)} %slice_bitcast_fusion.1), channel_id=1, source_target_pairs={{0,1},{2,3},{4,5},{6,7},{8,9},{10,11},{12,13},{14,15},{16,17},{18,... | collective-permute-start | bytes 1572872 | tf_op jit(solution)/shard_map/ppermute | solution.py:269
  147.1 17.0 %collective-permute-start.2 = (f32[1024,1024]{1,0:T(8,128)}, f32[1024,1024]{1,0:T(8,128)}, u32[]{:S(2)}, u32[]{:S(2)}) collective-permute-start(f32[1024,1024]{1,0:T(8,128)} %fusion), channel_id=1, source_target_pairs={{0,1},{1,0},{2,3},{3,2},{4,5},{5,4},{6,7},{7,6},{8,9},{9,8},{10,11... | collective-permute-start | bytes 12582920 | tf_op jit(solution)/shard_map/ppermute | solution.py:275
  164.1 60.9 %collective-permute-start.1 = (f32[1024,1024]{1,0:T(8,128)S(1)}, f32[1024,1024]{1,0:T(8,128)S(1)}, u32[]{:S(2)}, u32[]{:S(2)}) collective-permute-start(f32[1024,1024]{1,0:T(8,128)S(1)} %fusion.1), channel_id=1, source_target_pairs={{0,1},{1,0},{2,3},{3,2},{4,5},{5,4},{6,7},{7,6},{8,9},{9,8},{10,11... | collective-permute-start | bytes 12582920 | tf_op jit(solution)/shard_map/ppermute | solution.py:278
  168.6 56.4 %copy-start = (f32[1024,1024]{1,0:T(8,128)S(1)}, f32[1024,1024]{1,0:T(8,128)}, u32[]{:S(2)}) copy-start(f32[1024,1024]{1,0:T(8,128)} %get-tuple-element.7) | copy-start | bytes 12582916
  168.6 56.4 %copy-start.1 = (f32[4,256,1024]{2,1,0:T(8,128)S(1)}, f32[4,256,1024]{2,1,0:T(8,128)}, u32[]{:S(2)}) copy-start(f32[4,256,1024]{2,1,0:T(8,128)} %param.2) | copy-start | bytes 12582916

commit v3 on v2

--- a/solution.py
+++ b/solution.py
@@ -9,7 +9,8 @@
 MESH = pl.DeviceIdType.MESH
 HIGH = lax.Precision.HIGH
 TILE = 128
-CHUNKS = 4
+CHUNKS = 8
+LAG = 2
 
 
 def gather_kernel(groups, peers, f_ref, p_ref, t_ref, d_ref, local_sem, z_send, z_recv, g_send, g_recv):
@@ -31,8 +32,10 @@
     def greet(who):
         pl.semaphore_signal(barrier, inc=1, device_id=(who, layer), device_id_type=MESH)
 
-    for k in range(1, peers):
-        greet(base + lax.rem(place + k, peers))
+    beside = (place + 1 - 2 * lax.rem(place, 2), lax.rem(place + 2, peers))
+    across = lax.rem(beside[0] + 2, peers)
+    for who in beside:
+        greet(base + who)
 
     @pl.when(has_prev)
     def _():
@@ -42,7 +45,7 @@
     def _():
         greet(following)
 
-    pl.semaphore_wait(barrier, peers - 1 + has_prev.astype(jnp.int32) + has_next.astype(jnp.int32))
+    pl.semaphore_wait(barrier, 2 + has_prev.astype(jnp.int32) + has_next.astype(jnp.int32))
 
     def piece(a, dst, owner, c):
         if a == 0:
@@ -55,19 +58,11 @@
             send_sem=z_send.at[a, c], recv_sem=z_recv.at[a, c],
             device_id=(following, layer), device_id_type=MESH)
 
-    def spread(a, dst, c, k):
-        to = base + lax.rem(place + k, peers)
+    def send(a, dst, c, owner, to, k):
         return pltpu.make_async_remote_copy(
-            src_ref=piece(a, dst, place, c), dst_ref=piece(a, dst, place, c),
+            src_ref=piece(a, dst, owner, c), dst_ref=piece(a, dst, owner, c),
             send_sem=g_send.at[a, c, k], recv_sem=g_recv.at[a, c, k],
-            device_id=(to, layer), device_id_type=MESH)
-
-    def arrival(a, dst, c, k):
-        src = lax.rem(place + peers - k, peers)
-        return pltpu.make_async_remote_copy(
-            src_ref=piece(a, dst, src, c), dst_ref=piece(a, dst, src, c),
-            send_sem=g_send.at[a, c, k], recv_sem=g_recv.at[a, c, k],
-            device_id=(base + src, layer), device_id_type=MESH)
+            device_id=(base + to, layer), device_id_type=MESH)
 
     work = ((0, f_ref, t_ref), (1, p_ref, d_ref))
     steps = [(a, dst, c) for c in range(max(CHUNKS, peers))
@@ -90,8 +85,8 @@
         for item in work:
             own(*item).wait()
 
-    for a, dst, c in steps:
-        def step(a=a, dst=dst, c=c):
+    def issue(a, dst, c):
+        def body():
             @pl.when(has_prev)
             def _():
                 chain(a, dst, c).wait_recv()
@@ -100,24 +95,41 @@
             def _():
                 chain(a, dst, c).start()
 
-            for k in range(1, peers):
-                spread(a, dst, c, k).start()
-
-        when_used(a, place, c, step)
-
-    for a, dst, c in steps:
-        def finish(a=a, dst=dst, c=c):
-            for k in range(1, peers):
-                spread(a, dst, c, k).wait_send()
+            for k in range(2):
+                send(a, dst, c, place, beside[k], k).start()
+
+        when_used(a, place, c, body)
+
+    def forward(a, dst, c):
+        for k in range(2):
+            def body(k=k):
+                send(a, dst, c, beside[k], beside[k], k).wait_recv()
+                if c % 2 == k:
+                    send(a, dst, c, beside[k], beside[1 - k], 2).start()
+
+            when_used(a, beside[k], c, body)
+
+    def finish(a, dst, c):
+        def own_sent():
+            for k in range(2):
+                send(a, dst, c, place, beside[k], k).wait_send()
 
             @pl.when(has_next)
             def _():
                 chain(a, dst, c).wait_send()
 
-        when_used(a, place, c, finish)
-        for k in range(1, peers):
-            src = lax.rem(place + peers - k, peers)
-            when_used(a, src, c, lambda a=a, dst=dst, c=c, k=k: arrival(a, dst, c, k).wait_recv())
+        when_used(a, place, c, own_sent)
+        k = c % 2
+        when_used(a, beside[k], c, lambda: send(a, dst, c, beside[k], beside[1 - k], 2).wait_send())
+        when_used(a, across, c, lambda: send(a, dst, c, across, across, 2).wait_recv())
+
+    for i in range(len(steps) + LAG):
+        if i < len(steps):
+            issue(*steps[i])
+        if i >= LAG:
+            forward(*steps[i - LAG])
+    for item in steps:
+        finish(*item)
 
 
 def gather(groups, peers, f, p):

time: 244 us -> 225 us (0.922)
  Pallas kernels: 184 us -> 166 us
    pallas_call x1, Pallas kernels: 128 us -> 110 us  [gather(): pl.pallas_call(functools.partial(gather_kernel, groups, peers), out_shape...]
  transfers between devices with their start and end apart: 3 -> 3, of which waited for: 1 -> 1; matrix products, arithmetic and copies ran while one was open for 7% -> 8% of each run, Pallas kernels for 23% -> 25%
where the time goes in v3:
time: 225 us; the launch traced here: 223 us
  Pallas kernels  166 us (74%)
  matrix products  40.5 us (18%)
  starting transfers between devices  6.56 us (3%)
  other arithmetic  6.31 us (3%)
  local copies, waits for them, and re-layouts  3.49 us (2%)
    pallas_call x1, Pallas kernels, gather(): pl.pallas_call(functools.partial(gather_kernel, groups, peers), out_shape...  110 us
    pallas_call x1, Pallas kernels, factor_inverse(): pl.pallas_call(inverse_kernel, out_shape=jax.ShapeDtypeStruct((size, size...  56.4 us
    dot_general x4, matrix products, dot_t(): lax.dot_general(a, b, (((1,), (1,)), ((), ())), precision=HIGH, preferred...  40.5 us
    ppermute x1, starting transfers between devices, shards(): diag_block = square + lax.ppermute(square, 'layers', swap)  5.18 us
  transfers between devices with their start and end apart: 3, of which 1 were waited for; matrix products, arithmetic and copies ran while one was open for 8% of the time, Pallas kernels for 25%

profile of v3, /device:TPU:25, one launch (start us, length us, event | category | flops | bytes accessed | tf_op | source)
XLA Modules:
  0.0 223.5 jit_solution(2005518714316039650)
XLA Ops:
  0.0 1.1 slice_bitcast_fusion.1
  1.1 1.3 collective-permute-start
  2.4 0.1 broadcast_in_dim.28
  2.5 2.3 %slice_bitcast_fusion.f_ref = f32[256,1024]{1,0:T(8,128)} fusion(f32[8,256,1024]{2,1,0:T(8,128)} %param.3), kind=kLoop, calls=%fused_computation.9 | loop fusion | bytes 2097152 | tf_op jit(solution)/shard_map/squeeze | solution.py:283
  4.8 0.1 collective-permute-done
  4.9 1.9 bitcast_select_fusion.1.p_ref
  6.8 110.0 %shard_map.28 = (f32[1024,1024]{1,0:T(8,128)}, f32[512,1024]{1,0:T(8,128)}) custom-call(f32[256,1024]{1,0:T(8,128)} %slice_bitcast_fusion.f_ref, f32[128,1024]{1,0:T(8,128)} %bitcast_select_fusion.1.p_ref), custom_call_target="tpu_custom_call" | custom-call | tf_op jit(solution)/shard_map/pallas_call | solution.py:141
  116.8 12.3 %fusion = f32[1024,1024]{1,0:T(8,128)} fusion(f32[4,128,1024]{2,1,0:T(8,128)} %bitcast.31, pred[1024]{0:T(1024)(128)(4,1)S(1)} %broadcast_in_dim.29, f32[1024,1024]{1,0:T(8,128)} %get-tuple-element.7), kind=kOutput, calls=%fused_computation.1 | convolution fusion | flops 6444548096 | bytes 10486784 | tf_op jit(solution)/shard_map/dot_general | solution.py:272
  129.1 5.2 %collective-permute-start.2 = (f32[1024,1024]{1,0:T(8,128)}, f32[1024,1024]{1,0:T(8,128)}, u32[]{:S(2)}, u32[]{:S(2)}) collective-permute-start(f32[1024,1024]{1,0:T(8,128)} %fusion), channel_id=1, source_target_pairs={{0,1},{1,0},{2,3},{3,2},{4,5},{5,4},{6,7},{7,6},{8,9},{9,8},{10,11... | collective-permute-start | bytes 12582920 | tf_op jit(solution)/shard_map/ppermute | solution.py:287
  134.3 10.5 %fusion.1 = f32[1024,1024]{1,0:T(8,128)S(1)} fusion(f32[1024,1024]{1,0:T(8,128)} %get-tuple-element.7, f32[2,1024,1024]{2,1,0:T(8,128)} %bitcast.29, s32[]{:T(128)S(6)} %select_n.23), kind=kOutput, calls=%fused_computation.2 | convolution fusion | flops 6442450944 | bytes 12582916 | tf_op jit(solution)/shard_map/dot_general | solution.py:272
  144.8 0.1 collective-permute-start.1
  144.9 0.0 collective-permute-done.2
  144.9 4.4 %add.17.d_ref = f32[1024,1024]{1,0:T(8,128)S(1)} add(f32[1024,1024]{1,0:T(8,128)} %fusion, f32[1024,1024]{1,0:T(8,128)} %collective-permute-done.2) | non-fusion elementwise | flops 1048576 | bytes 12582912 | tf_op jit(solution)/shard_map/add | solution.py:287
  149.3 0.0 copy-start
  149.3 0.0 copy-start.1
  149.3 56.4 %shard_map.29 = f32[1024,1024]{1,0:T(8,128)S(1)} custom-call(f32[1024,1024]{1,0:T(8,128)S(1)} %add.17.d_ref), custom_call_target="tpu_custom_call" | custom-call | flops 64424509440 | bytes 8388608 | tf_op jit(solution)/shard_map/pallas_call | solution.py:260
  205.7 0.0 collective-permute-done.1
  205.7 0.0 copy-done
  205.7 0.0 copy-done.1
  205.7 9.4 %bitcast_subtract_fusion = f32[1024,1024]{1,0:T(8,128)S(1)} fusion(f32[4,256,1024]{2,1,0:T(8,128)S(1)} %copy-done.1, f32[1024,1024]{1,0:T(8,128)S(1)} %collective-permute-done.1, f32[1024,1024]{1,0:T(8,128)S(1)} %copy-done, f32[2,1024,1024]{2,1,0:T(8,128)} %bitcast.30, s32[]{:T(128)S(6)} %select_n.20), kind=kOutput, calls=%fused_computation.6 | convolution fusion | flops 6444548096 | bytes 20971524 | tf_op jit(solution)/shard_map/dot_general | solution.py:272
  215.1 8.3 %fusion.11 = f32[1024,1024]{1,0:T(8,128)} fusion(f32[1024,1024]{1,0:T(8,128)S(1)} %bitcast_subtract_fusion, f32[1024,1024]{1,0:T(8,128)S(1)} %shard_map.29), kind=kOutput, calls=%fused_computation.15 | convolution fusion | flops 6442450944 | bytes 12582912 | tf_op jit(solution)/shard_map/dot_general | solution.py:272
  (2 shorter events, 0.0 us)
Async XLA Ops:
  1.1 3.8 %collective-permute-start = (f32[128,1024]{1,0:T(8,128)S(1)}, f32[128,1024]{1,0:T(8,128)S(1)}, u32[]{:S(2)}, u32[]{:S(2)}) collective-permute-start(f32[128,1024]{1,0:T(8,128)S(1)} %slice_bitcast_fusion.1), channel_id=1, source_target_pairs={{0,1},{2,3},{4,5},{6,7},{8,9},{10,11},{12,13},{14,15},{16,17},{18,... | collective-permute-start | bytes 1572872 | tf_op jit(solution)/shard_map/ppermute | solution.py:281
  129.1 15.8 %collective-permute-start.2 = (f32[1024,1024]{1,0:T(8,128)}, f32[1024,1024]{1,0:T(8,128)}, u32[]{:S(2)}, u32[]{:S(2)}) collective-permute-start(f32[1024,1024]{1,0:T(8,128)} %fusion), channel_id=1, source_target_pairs={{0,1},{1,0},{2,3},{3,2},{4,5},{5,4},{6,7},{7,6},{8,9},{9,8},{10,11... | collective-permute-start | bytes 12582920 | tf_op jit(solution)/shard_map/ppermute | solution.py:287
  144.8 60.9 %collective-permute-start.1 = (f32[1024,1024]{1,0:T(8,128)S(1)}, f32[1024,1024]{1,0:T(8,128)S(1)}, u32[]{:S(2)}, u32[]{:S(2)}) collective-permute-start(f32[1024,1024]{1,0:T(8,128)S(1)} %fusion.1), channel_id=1, source_target_pairs={{0,1},{1,0},{2,3},{3,2},{4,5},{5,4},{6,7},{7,6},{8,9},{9,8},{10,11... | collective-permute-start | bytes 12582920 | tf_op jit(solution)/shard_map/ppermute | solution.py:290
  149.3 56.4 %copy-start = (f32[1024,1024]{1,0:T(8,128)S(1)}, f32[1024,1024]{1,0:T(8,128)}, u32[]{:S(2)}) copy-start(f32[1024,1024]{1,0:T(8,128)} %get-tuple-element.7) | copy-start | bytes 12582916
  149.3 56.4 %copy-start.1 = (f32[4,256,1024]{2,1,0:T(8,128)S(1)}, f32[4,256,1024]{2,1,0:T(8,128)}, u32[]{:S(2)}) copy-start(f32[4,256,1024]{2,1,0:T(8,128)} %param.2) | copy-start | bytes 12582916

commit v4 on v3

--- a/solution.py
+++ b/solution.py
@@ -9,7 +9,7 @@
 MESH = pl.DeviceIdType.MESH
 HIGH = lax.Precision.HIGH
 TILE = 128
-CHUNKS = 8
+CHUNKS = 16
 LAG = 2
 
 
@@ -23,7 +23,7 @@
     has_next = group < groups - 1
     prev = jnp.where(has_prev, row - peers, row)
     following = jnp.where(has_next, row + peers, row)
-    heights = (f_ref.shape[0], p_ref.shape[0])
+    heights = (f_ref.shape[1], p_ref.shape[0])
     part = heights[0] // CHUNKS
     wide = p_ref.shape[1] // peers
 
@@ -64,7 +64,7 @@
             send_sem=g_send.at[a, c, k], recv_sem=g_recv.at[a, c, k],
             device_id=(base + to, layer), device_id_type=MESH)
 
-    work = ((0, f_ref, t_ref), (1, p_ref, d_ref))
+    work = ((0, f_ref.at[0], t_ref), (1, p_ref, d_ref))
     steps = [(a, dst, c) for c in range(max(CHUNKS, peers))
              for a, dst in ((0, t_ref), (1, d_ref)) if c < (CHUNKS, peers)[a]]
 
@@ -133,7 +133,7 @@
 
 
 def gather(groups, peers, f, p):
-    rows, cols = f.shape
+    rows, cols = f.shape[1:]
     out = jax.ShapeDtypeStruct((peers * rows, cols), f.dtype)
     out_p = jax.ShapeDtypeStruct((peers * p.shape[0], p.shape[1]), p.dtype)
     count = max(CHUNKS, peers)
@@ -229,10 +229,10 @@
     return jnp.concatenate(x, 0)
 
 
-def inverse_kernel(d_ref, o_ref, m_ref):
+def inverse_kernel(d_ref, e_ref, o_ref, m_ref):
     size = d_ref.shape[0]
     count = size // TILE
-    m_ref[...] = d_ref[...]
+    m_ref[...] = d_ref[...] + e_ref[...]
     col_tile = lax.broadcasted_iota(jnp.int32, (TILE, size), 1) // TILE
     eye = (lax.broadcasted_iota(jnp.int32, (TILE, TILE), 0)
            == lax.broadcasted_iota(jnp.int32, (TILE, TILE), 1)).astype(jnp.float32)
@@ -255,17 +255,17 @@
             m_ref[there, :] = old - dot3(split(left), u_parts)
 
 
-def factor_inverse(d):
+def factor_inverse(d, e):
     size = d.shape[0]
     return pl.pallas_call(
         inverse_kernel,
         out_shape=jax.ShapeDtypeStruct((size, size), jnp.float32),
-        in_specs=[pl.BlockSpec(memory_space=pltpu.VMEM)],
+        in_specs=[pl.BlockSpec(memory_space=pltpu.VMEM)] * 2,
         out_specs=pl.BlockSpec(memory_space=pltpu.VMEM),
         scratch_shapes=[pltpu.VMEM((size, size), jnp.float32)],
         compiler_params=pltpu.CompilerParams(vmem_limit_bytes=32 * 1024 * 1024),
         cost_estimate=pl.CostEstimate(flops=size ** 3 * 60, bytes_accessed=8 * size * size, transcendentals=0),
-    )(d)
+    )(d, e)
 
 
 def dot_t(a, b):
@@ -280,16 +280,16 @@
     half = row_block // 2
     second = lax.ppermute(panel[0, half:], "layers", [(0, 1)])
     share = jnp.where(layer == 0, panel[0, :half], second)
-    target, diag_share = gather(rows_count // peers, peers, factor[0], share)
+    target, diag_share = gather(rows_count // peers, peers, factor, share)
     slot = lax.broadcasted_iota(jnp.int32, (1, 2, 1, 1), 1) == layer
     diag_input = jnp.where(slot, diag_share.reshape(peers, 1, half, width), 0.0).reshape(width, width)
     square = diag_input - dot_t(target, target)
-    diag_block = square + lax.ppermute(square, "layers", swap)
+    from_square = lax.ppermute(square, "layers", swap)
     flat = factor.reshape(2, own_cycles * row_block, factor.shape[2])
     other = dot_t(lax.dynamic_index_in_dim(flat, 1 - layer, 0, False), target)
     from_other = lax.ppermute(other, "layers", swap)
     mine = dot_t(lax.dynamic_index_in_dim(flat, layer, 0, False), target)
-    inverse = factor_inverse(diag_block)
+    inverse = factor_inverse(square, from_square)
     reduced = panel.reshape(-1, width) - (mine + from_other)
     return dot_t(reduced, inverse).reshape(panel.shape)
 

time: 225 us -> 227 us (level)
  Pallas kernels: 166 us -> 173 us
  other arithmetic: 6.31 us -> 1.9 us
  local copies, waits for them, and re-layouts: 3.49 us -> 1.18 us
  waiting for transfers between devices: 0.09 us -> 2.4 us
    add x1 -> x0, other arithmetic: 4.4 us -> none  [shards(): diag_block = square + lax.ppermute(square, 'layers', swap)]
    pallas_call x1, Pallas kernels: 56.4 us -> 59.9 us  [factor_inverse(): pl.pallas_call(inverse_kernel, out_shape=jax.ShapeDtypeStruct((size, size...]
    pallas_call x1, Pallas kernels: 110 us -> 113 us  [gather(): pl.pallas_call(functools.partial(gather_kernel, groups, peers), out_shape...]
    ppermute x1, waiting for transfers between devices: 0.08 us -> 2.39 us  [shards(): second = lax.ppermute(panel[0, half:], 'layers', [(0, 1)])]
    squeeze x1 -> x0, local copies, waits for them, and re-layouts: 2.31 us -> none  [shards(): target, diag_share = gather(rows_count // peers, peers, factor[0], share)]
  transfers between devices with their start and end apart: 3 -> 3, of which waited for: 1 -> 1; matrix products, arithmetic and copies ran while one was open for 8% -> 5% of each run, Pallas kernels for 25% -> 26%
where the time goes in v4:
time: 227 us
  Pallas kernels  173 us (76%)
  matrix products  42.4 us (19%)
  starting transfers between devices  5.77 us (3%)
  waiting for transfers between devices  2.4 us (1%)
    pallas_call x1, Pallas kernels, gather(): pl.pallas_call(functools.partial(gather_kernel, groups, peers), out_shape...  113 us
    pallas_call x1, Pallas kernels, factor_inverse(): pl.pallas_call(inverse_kernel, out_shape=jax.ShapeDtypeStruct((size, size...  59.9 us
    dot_general x4, matrix products, dot_t(): lax.dot_general(a, b, (((1,), (1,)), ((), ())), precision=HIGH, preferred...  42.4 us
  transfers between devices with their start and end apart: 3, of which 1 were waited for; matrix products, arithmetic and copies ran while one was open for 5% of the time, Pallas kernels for 26%

profile of v4, /device:TPU:25, one launch (start us, length us, event | category | flops | bytes accessed | tf_op | source)
XLA Modules:
  0.0 226.6 jit_solution(10385149296772949633)
XLA Ops:
  0.0 1.1 slice_bitcast_fusion
  1.1 1.3 collective-permute-start
  2.4 0.1 broadcast_in_dim.28
  2.5 2.4 %collective-permute-done = f32[128,1024]{1,0:T(8,128)S(1)} collective-permute-done((f32[128,1024]{1,0:T(8,128)S(1)}, f32[128,1024]{1,0:T(8,128)S(1)}, u32[]{:S(2)}, u32[]{:S(2)}) %collective-permute-start) | collective-permute-done | bytes 524320 | tf_op jit(solution)/shard_map/ppermute | solution.py:281
  4.9 1.9 bitcast_select_fusion.1.p_ref
  6.8 112.8 %shard_map.28 = (f32[1024,1024]{1,0:T(8,128)}, f32[512,1024]{1,0:T(8,128)}) custom-call(f32[8,256,1024]{2,1,0:T(8,128)} %f_ref.1, f32[128,1024]{1,0:T(8,128)} %bitcast_select_fusion.1.p_ref), custom_call_target="tpu_custom_call" | custom-call | tf_op jit(solution)/shard_map/pallas_call | solution.py:141
  119.6 12.3 %fusion.d_ref = f32[1024,1024]{1,0:T(8,128)} fusion(f32[4,128,1024]{2,1,0:T(8,128)} %bitcast.31, pred[1024]{0:T(1024)(128)(4,1)S(1)} %broadcast_in_dim.29, f32[1024,1024]{1,0:T(8,128)} %get-tuple-element.7), kind=kOutput, calls=%fused_computation.1 | convolution fusion | flops 6444548096 | bytes 10486784 | tf_op jit(solution)/shard_map/dot_general | solution.py:272
  131.9 4.4 %collective-permute-start.2 = (f32[1024,1024]{1,0:T(8,128)}, f32[1024,1024]{1,0:T(8,128)}, u32[]{:S(2)}, u32[]{:S(2)}) collective-permute-start(f32[1024,1024]{1,0:T(8,128)} %fusion.d_ref), channel_id=1, source_target_pairs={{0,1},{1,0},{2,3},{3,2},{4,5},{5,4},{6,7},{7,6},{8,9},{9,8},{10,11... | collective-permute-start | bytes 12582920 | tf_op jit(solution)/shard_map/ppermute | solution.py:287
  136.4 0.0 slice-start
  136.4 11.6 %fusion.1 = f32[1024,1024]{1,0:T(8,128)} fusion(f32[1024,1024]{1,0:T(8,128)} %get-tuple-element.7, f32[2,1024,1024]{2,1,0:T(8,128)} %bitcast.27, s32[]{:T(128)S(6)} %select_n.23), kind=kOutput, calls=%fused_computation.2 | convolution fusion | flops 6442450944 | bytes 12582916 | tf_op jit(solution)/shard_map/dot_general | solution.py:272
  147.9 0.0 copy-start
  147.9 0.0 slice-start.1
  147.9 0.0 copy-start.1
  147.9 0.1 collective-permute-start.1
  148.0 0.0 collective-permute-done.2.e_ref
  148.0 59.9 %shard_map.29 = f32[1024,1024]{1,0:T(8,128)S(1)} custom-call(f32[1024,1024]{1,0:T(8,128)} %fusion.d_ref, f32[1024,1024]{1,0:T(8,128)} %collective-permute-done.2.e_ref), custom_call_target="tpu_custom_call" | custom-call | flops 64424509440 | bytes 8388608 | tf_op jit(solution)/shard_map/pallas_call | solution.py:260
  208.0 0.0 collective-permute-done.1
  208.0 0.0 slice-done
  208.0 0.0 copy-done
  208.0 0.0 slice-done.1
  208.0 0.0 copy-done.1
  208.0 10.2 %bitcast_subtract_fusion = f32[1024,1024]{1,0:T(8,128)S(1)} fusion(f32[4,256,1024]{2,1,0:T(8,128)S(1)} %copy-done.1, f32[1024,1024]{1,0:T(8,128)} %collective-permute-done.1, f32[1024,1024]{1,0:T(8,128)S(1)} %copy-done, f32[2,1024,1024]{2,1,0:T(8,128)S(1)} %bitcast.30, s32[]{:T(128)S(6)} %select_n.20), kind=kOutput, calls=%fused_computation.6 | convolution fusion | flops 6444548096 | bytes 20971524 | tf_op jit(solution)/shard_map/dot_general | solution.py:272
  218.2 8.3 %fusion.11 = f32[1024,1024]{1,0:T(8,128)} fusion(f32[1024,1024]{1,0:T(8,128)S(1)} %bitcast_subtract_fusion, f32[1024,1024]{1,0:T(8,128)S(1)} %shard_map.29), kind=kOutput, calls=%fused_computation.14 | convolution fusion | flops 6442450944 | bytes 12582912 | tf_op jit(solution)/shard_map/dot_general | solution.py:272
  (3 shorter events, 0.0 us)
Async XLA Ops:
  1.1 3.8 %collective-permute-start = (f32[128,1024]{1,0:T(8,128)S(1)}, f32[128,1024]{1,0:T(8,128)S(1)}, u32[]{:S(2)}, u32[]{:S(2)}) collective-permute-start(f32[128,1024]{1,0:T(8,128)S(1)} %slice_bitcast_fusion), channel_id=1, source_target_pairs={{0,1},{2,3},{4,5},{6,7},{8,9},{10,11},{12,13},{14,15},{16,17},{18,... | collective-permute-start | bytes 1572872 | tf_op jit(solution)/shard_map/ppermute | solution.py:281
  131.9 16.1 %collective-permute-start.2 = (f32[1024,1024]{1,0:T(8,128)}, f32[1024,1024]{1,0:T(8,128)}, u32[]{:S(2)}, u32[]{:S(2)}) collective-permute-start(f32[1024,1024]{1,0:T(8,128)} %fusion.d_ref), channel_id=1, source_target_pairs={{0,1},{1,0},{2,3},{3,2},{4,5},{5,4},{6,7},{7,6},{8,9},{9,8},{10,11... | collective-permute-start | bytes 12582920 | tf_op jit(solution)/shard_map/ppermute | solution.py:287
  136.4 71.6 %slice-start = ((s8[8388608]{0:T(1024)(128)(4,1)}), s8[4194304]{0:T(1024)(128)(4,1)S(1)}, s32[]{:S(2)}) async-start(s8[8388608]{0:T(1024)(128)(4,1)} %bitcast.28), calls=%async_computation | async-start | bytes 8388608
  147.9 60.1 %copy-start = (f32[1024,1024]{1,0:T(8,128)S(1)}, f32[1024,1024]{1,0:T(8,128)}, u32[]{:S(2)}) copy-start(f32[1024,1024]{1,0:T(8,128)} %get-tuple-element.7) | copy-start | bytes 12582916
  147.9 60.1 %slice-start.1 = ((s8[8388608]{0:T(1024)(128)(4,1)}), s8[4194304]{0:T(1024)(128)(4,1)S(1)}, s32[]{:S(2)}) async-start(s8[8388608]{0:T(1024)(128)(4,1)} %bitcast.28), calls=%async_computation.1 | async-start | bytes 8388608
  147.9 60.1 %copy-start.1 = (f32[4,256,1024]{2,1,0:T(8,128)S(1)}, f32[4,256,1024]{2,1,0:T(8,128)}, u32[]{:S(2)}) copy-start(f32[4,256,1024]{2,1,0:T(8,128)} %param.2) | copy-start | bytes 12582916
  147.9 60.0 %collective-permute-start.1 = (f32[1024,1024]{1,0:T(8,128)}, f32[1024,1024]{1,0:T(8,128)}, u32[]{:S(2)}, u32[]{:S(2)}) collective-permute-start(f32[1024,1024]{1,0:T(8,128)} %fusion.1), channel_id=1, source_target_pairs={{0,1},{1,0},{2,3},{3,2},{4,5},{5,4},{6,7},{7,6},{8,9},{9,8},{10,11... | collective-permute-start | bytes 12582920 | tf_op jit(solution)/shard_map/ppermute | solution.py:290
